TPU v7x, 256 devices: a whole 4x4x8 slice. The times are simulated.
256 devices in a mesh: dp: 2 (over core), head: 8 (over x, z_lo), ctx: 16 (over y, z_hi).
Axes of the slice: x: 4, y: 4, z: 8 (z_hi: 4, z_lo: 2; z = z_hi * 2 + z_lo), core: 2. Of those that a mesh axis runs over, the one named last changes fastest.
Arguments:
- query_states: bfloat16 [2, 16384, 32, 128], P('dp', 'ctx', 'head'), may hold values from -6 to 6
- key_states: bfloat16 [2, 16384, 8, 128], P('dp', 'ctx', 'head'), may hold values from -6 to 6
- value_states: bfloat16 [2, 16384, 8, 128], P('dp', 'ctx', 'head'), may hold values from -12 to 12
- gate_values: float32 [32], P('head'), may hold values from 0.1 to 0.9
- head_flags: int32 [32], P('head'), may hold values from 0 to 1, as said below
- output_grad: bfloat16 [2, 16384, 32, 128], P('dp', 'ctx', 'head'), may hold values from -16 to 16
Outputs:
- blended: bfloat16 [2, 16384, 32, 128], P('dp', 'ctx', 'head')
- gate_grad: float32 [32], replicated
Inputs may be any that keep to these rules, and one draw needn't show every extreme that they name: `head_flags`: exactly 1 of the 4 query heads of each key-value head have flag 1.
All inputs are finite; a program needn't handle non-finite values.
Results may differ from a plain program's by a relative error of at most 0.005.
Values may be sent and summed in bfloat16 or wider, within the bound.
No kernel may reach another device: no remote copies, remote signals or barrier semaphores. Data moves between devices by JAX's collectives and lax.ppermute only.
A program may use at most 64 MiB of HBM per device.

v0:
```python
import math

import jax
import jax.numpy as jnp
from jax import lax
from jax.sharding import PartitionSpec as P

RET = 1
SINK = 64
WINDOW = 2048


def from_behind(block, axis, distance):
    devices = range(lax.axis_size(axis))
    route = [(i - distance, i) for i in devices if i - distance in devices]
    return lax.ppermute(block, axis, route)


def empty_state(row_count, groups, heads, width):
    return (
        jnp.full((row_count, groups, heads), -jnp.inf, jnp.float32),
        jnp.zeros((row_count, groups, heads), jnp.float32),
        jnp.zeros((row_count, groups, heads, width), jnp.float32),
    )


def block_update(carried, query_block, key_rows, value_rows, allowed):
    running_max, running_sum, running_acc = carried
    scaling = 1.0 / math.sqrt(query_block.shape[-1])
    scores = (
        jnp.einsum("rgeh,kgh->rgek", query_block, key_rows, preferred_element_type=jnp.float32)
        * scaling
    )
    visible = allowed[:, None, None, :]
    scores = jnp.where(visible, scores, -jnp.inf)
    newest = jnp.maximum(running_max, jnp.max(scores, axis=-1))
    anchor = jnp.where(newest == -jnp.inf, 0.0, newest)
    factor = jnp.exp(running_max - anchor)
    weights = jnp.where(visible, jnp.exp(scores - anchor[..., None]), 0.0)
    running_sum = running_sum * factor + jnp.sum(weights, axis=-1)
    update = jnp.einsum(
        "rgek,kgh->rgeh",
        weights.astype(jnp.bfloat16),
        value_rows,
        preferred_element_type=jnp.float32,
    )
    running_acc = running_acc * factor[..., None] + update
    return (newest, running_sum, running_acc)


def sweep_blocks(carried, queries, positions, key_rows, value_rows, key_first, needed, allowed_fn):
    row_count = queries.shape[0]
    key_count = key_rows.shape[0]
    row_block = math.gcd(row_count, 512)
    key_block = math.gcd(key_count, 512)
    key_steps = key_count // key_block
    total_steps = row_count // row_block * key_steps

    def visit_block(counter, current):
        row_at = counter // key_steps * row_block
        key_at = counter % key_steps * key_block
        row_pos = lax.dynamic_slice_in_dim(positions, row_at, row_block)
        key_pos = key_first + key_at + jnp.arange(key_block, dtype=jnp.int32)

        def compute(present):
            portion = tuple(
                (lax.dynamic_slice_in_dim(member, row_at, row_block) for member in present)
            )
            renewed = block_update(
                portion,
                lax.dynamic_slice_in_dim(queries, row_at, row_block),
                lax.dynamic_slice_in_dim(key_rows, key_at, key_block),
                lax.dynamic_slice_in_dim(value_rows, key_at, key_block),
                allowed_fn(row_pos[:, None], key_pos[None, :]),
            )
            return tuple(
                (
                    lax.dynamic_update_slice_in_dim(member, fresh_part, row_at, 0)
                    for member, fresh_part in zip(present, renewed)
                )
            )

        def unchanged(present):
            return present

        return lax.cond(
            needed(row_pos[0], row_pos[row_block - 1], key_pos[0], key_pos[key_block - 1]),
            compute,
            unchanged,
            current,
        )

    return lax.fori_loop(0, total_steps, visit_block, carried)


def causal_needed(row_low, row_high, key_low, key_high):
    return key_low <= row_high


def causal_allowed(row_pos, key_pos):
    return key_pos <= row_pos


def window_needed(row_low, row_high, key_low, key_high):
    return (key_low <= row_high) & (key_high > row_low - WINDOW)


def window_allowed(row_pos, key_pos):
    return (key_pos >= 0) & (key_pos <= row_pos) & (row_pos - key_pos < WINDOW)


def sinks_needed(row_low, row_high, key_low, key_high):
    return (key_low < SINK) & (row_high - key_low >= WINDOW)


def sinks_allowed(row_pos, key_pos):
    return (key_pos < SINK) & (key_pos <= row_pos) & (row_pos - key_pos >= WINDOW)


def on_device(query_states, key_states, value_states, gate_values, head_flags, output_grad):
    tok_rows = query_states.shape[1]
    groups = key_states.shape[2]
    head_dim = key_states.shape[3]
    per_group = query_states.shape[2] // groups
    ctx_count = lax.axis_size("ctx")
    ctx_index = lax.axis_index("ctx")
    queries = query_states[0].reshape(tok_rows, groups, per_group, head_dim)
    stacked = jnp.stack([key_states[0], value_states[0]])
    marked = head_flags.reshape(groups, per_group)
    ordinal = jnp.cumsum(marked, axis=1) - 1
    slot_ids = jnp.arange(RET, dtype=jnp.int32)
    picker = ((marked[:, None, :] == 1) & (ordinal[:, None, :] == slot_ids[None, :, None])).astype(
        jnp.float32
    )
    chosen = jnp.einsum(
        "gre,tgeh->tgrh", picker.astype(jnp.bfloat16), queries, preferred_element_type=jnp.float32
    ).astype(jnp.bfloat16)
    own_pos = ctx_index * tok_rows + jnp.arange(tok_rows, dtype=jnp.int32)
    full_state = empty_state(tok_rows, groups, RET, head_dim)
    near_state = empty_state(tok_rows, groups, per_group, head_dim)
    portion = lax.all_gather(stacked, "ctx", axis=1, tiled=True)
    start = jnp.int32(0)
    full_now = sweep_blocks(
        full_state, chosen, own_pos, portion[0], portion[1], start, causal_needed, causal_allowed
    )
    head_rows = min(SINK, portion.shape[1])
    sink_part = portion[:, :head_rows]

    def with_sinks(present):
        return sweep_blocks(
            present,
            queries,
            own_pos,
            sink_part[0],
            sink_part[1],
            start,
            sinks_needed,
            sinks_allowed,
        )

    def without_sinks(present):
        return present

    near_now = lax.cond(start < SINK, with_sinks, without_sinks, near_state)
    near_state = near_now
    reach_depth = min((WINDOW - 1) // tok_rows + 1, ctx_count - 1)
    earlier = [from_behind(stacked, "ctx", distance) for distance in range(reach_depth, 0, -1)]
    near_keys = jnp.concatenate(earlier + [stacked], axis=1)
    near_state = sweep_blocks(
        near_state,
        queries,
        own_pos,
        near_keys[0],
        near_keys[1],
        (ctx_index - reach_depth) * tok_rows,
        window_needed,
        window_allowed,
    )
    full_out = full_now[2] / full_now[1][..., None]
    near_out = near_state[2] / near_state[1][..., None]
    full_heads = jnp.einsum("gre,tgrh->tgeh", picker, full_out, precision=lax.Precision.HIGHEST)
    gate_cols = gate_values.reshape(groups, per_group)[None, :, :, None]
    retrieval = (marked == 1)[None, :, :, None]
    mixed = jnp.where(retrieval, gate_cols * full_heads + (1.0 - gate_cols) * near_out, near_out)
    blended = mixed.astype(jnp.bfloat16).reshape(1, tok_rows, groups * per_group, head_dim)
    grad_rows = output_grad[0].reshape(tok_rows, groups, per_group, head_dim).astype(jnp.float32)
    local_terms = jnp.sum(grad_rows * (full_heads - near_out), axis=(0, 3)) * marked.astype(
        jnp.float32
    )
    heads_dev = groups * per_group
    padded = lax.dynamic_update_slice_in_dim(
        jnp.zeros((heads_dev * lax.axis_size("head"),), jnp.float32),
        local_terms.reshape(heads_dev),
        lax.axis_index("head") * heads_dev,
        0,
    )
    totals = lax.psum(padded, ("dp", "head", "ctx"))
    normalizer = 1.0 / math.sqrt(
        lax.axis_size("dp") * query_states.shape[0] * tok_rows * ctx_count * head_dim
    )
    return (blended, totals * normalizer)


def solution(mesh):
    return jax.shard_map(
        on_device,
        mesh=mesh,
        in_specs=(
            P("dp", "ctx", "head", None),
            P("dp", "ctx", "head", None),
            P("dp", "ctx", "head", None),
            P("head"),
            P("head"),
            P("dp", "ctx", "head", None),
        ),
        out_specs=(P("dp", "ctx", "head", None), P()),
        check_vma=False,
    )
```

profile of v0, /device:TPU:1, one launch (start us, length us, event | category | flops | bytes accessed | tf_op | source)
XLA Modules:
  0.0 829.5 jit_solution(2054756737701288816)
XLA Ops:
  10.1 5.8 collective-permute-start.1
  15.9 7.8 collective-permute-start
  25.9 1.5 copy.29
  28.1 3.1 collective-permute-done.1
  31.2 24.1 %collective-permute-done = bf16[2,1024,1,128]{3,1,2,0:T(8,128)(2,1)} collective-permute-done((bf16[2,1024,1,128]{3,1,2,0:T(8,128)(2,1)}, bf16[2,1024,1,128]{3,1,2,0:T(8,128)(2,1)}, u32[]{:S(2)}, u32[]{:S(2)}) %collective-permute-start) | collective-permute-done | bytes 524320 | tf_op jit(solution)/shard_map/ppermute | solution.py:16
  57.4 1.2 copy.24
  58.6 96.1 %all-gather.2.cloned.1.call-done = bf16[2,16384,1,128]{3,1,2,0:T(8,128)(2,1)} async-done(((bf16[2,1024,1,128]{3,1,2,0:T(8,128)(2,1)}), bf16[2,16384,1,128]{3,1,2,0:T(8,128)(2,1)}) %all-gather.2.cloned.1.call-update) | async-done | bytes 8388624 | tf_op jit(solution)/shard_map/all_gather | solution.py:141
  154.6 5.7 slice_bitcast_fusion
  160.4 183.1 %while.58 = (s32[]{:T(128)}, f32[1024,1,1]{0,2,1:T(1,128)S(1)}, f32[1024,1,1]{0,2,1:T(1,128)S(1)}, f32[1024,1,1,128]{0,3,2,1:T(8,128)S(1)}, s32[1024]{0:T(1024)S...) while((s32[]{:T(128)}, f32[1024,1,1]{0,2,1:T(1,128)S(1)}, ...), condition=%wide.region_6.7_spmd, body=%wide.region_1.6_spmd.sunk | while | flops 137498128 | bytes 4645472 | solution.py:93
  163.1 3.7 conditional.6
  163.1 1.2 fusion.78
  164.8 1.3 fusion.1
  252.9 3.6 conditional.6
  252.9 1.2 fusion.78
  254.5 1.3 fusion.1
  259.2 3.6 conditional.6
  259.2 1.2 fusion.78
  260.9 1.3 fusion.1
  345.5 3.1 while.59
  348.5 1.8 copy.23
  350.4 158.5 %while.60 = (s32[]{:T(128)}, f32[1024,1,4]{0,2,1:T(4,128)S(1)}, f32[1024,1,4]{0,2,1:T(4,128)S(1)}, f32[1024,1,4,128]{0,3,2,1:T(8,128)}, s32[]{:T(128)}, /*index=...) while((s32[]{:T(128)}, f32[1024,1,4]{0,2,1:T(4,128)S(1)}, ...), condition=%wide.region_18.19_spmd, body=%wide.region_13.18_spmd.sunk | while | flops 552356864 | bytes 27178672 | solution.py:93
  353.4 12.6 %conditional.8 = ((f32[1024,1,4]{0,2,1:T(4,128)S(1)}, f32[1024,1,4]{0,2,1:T(4,128)S(1)}, f32[1024,1,4,128]{0,3,2,1:T(8,128)})) conditional(s32[]{:T(128)} %bitcast.205, (f32[1024,1,4]{0,2,1:T(4,128)S(1)}, f32[1024,1,4]{0,2,1:T(4,128)S(1)}, f32[1024,1,4,128]{0,3,2,1:T(8,128)}) %tuple.164, (s32[]{:T(128)}, f32[1024,1,4]{0,2,1:T(4,128)S(1)}, ...), branch_computations={%region_14.14_spmd, %region_15.17_spmd} | conditional | flops 552356352 | bytes 27172004 | solution.py:86
  353.9 1.9 fusion.41
  357.3 2.3 fusion.51
  360.3 5.7 dynamic_update_slice.31
  369.1 12.6 %conditional.8 = ((f32[1024,1,4]{0,2,1:T(4,128)S(1)}, f32[1024,1,4]{0,2,1:T(4,128)S(1)}, f32[1024,1,4,128]{0,3,2,1:T(8,128)})) conditional(s32[]{:T(128)} %bitcast.205, (f32[1024,1,4]{0,2,1:T(4,128)S(1)}, f32[1024,1,4]{0,2,1:T(4,128)S(1)}, f32[1024,1,4,128]{0,3,2,1:T(8,128)}) %tuple.164, (s32[]{:T(128)}, f32[1024,1,4]{0,2,1:T(4,128)S(1)}, ...), branch_computations={%region_14.14_spmd, %region_15.17_spmd} | conditional | flops 552356352 | bytes 27172004 | solution.py:86
  369.5 1.9 fusion.41
  373.0 2.3 fusion.51
  376.0 5.7 dynamic_update_slice.31
  384.8 12.6 %conditional.8 = ((f32[1024,1,4]{0,2,1:T(4,128)S(1)}, f32[1024,1,4]{0,2,1:T(4,128)S(1)}, f32[1024,1,4,128]{0,3,2,1:T(8,128)})) conditional(s32[]{:T(128)} %bitcast.205, (f32[1024,1,4]{0,2,1:T(4,128)S(1)}, f32[1024,1,4]{0,2,1:T(4,128)S(1)}, f32[1024,1,4,128]{0,3,2,1:T(8,128)}) %tuple.164, (s32[]{:T(128)}, f32[1024,1,4]{0,2,1:T(4,128)S(1)}, ...), branch_computations={%region_14.14_spmd, %region_15.17_spmd} | conditional | flops 552356352 | bytes 27172004 | solution.py:86
  385.2 1.9 fusion.41
  388.6 2.3 fusion.51
  391.6 5.7 dynamic_update_slice.31
  400.4 12.6 %conditional.8 = ((f32[1024,1,4]{0,2,1:T(4,128)S(1)}, f32[1024,1,4]{0,2,1:T(4,128)S(1)}, f32[1024,1,4,128]{0,3,2,1:T(8,128)})) conditional(s32[]{:T(128)} %bitcast.205, (f32[1024,1,4]{0,2,1:T(4,128)S(1)}, f32[1024,1,4]{0,2,1:T(4,128)S(1)}, f32[1024,1,4,128]{0,3,2,1:T(8,128)}) %tuple.164, (s32[]{:T(128)}, f32[1024,1,4]{0,2,1:T(4,128)S(1)}, ...), branch_computations={%region_14.14_spmd, %region_15.17_spmd} | conditional | flops 552356352 | bytes 27172004 | solution.py:86
  400.8 1.9 fusion.41
  404.3 2.3 fusion.51
  407.3 5.7 dynamic_update_slice.31
  416.1 12.6 %conditional.8 = ((f32[1024,1,4]{0,2,1:T(4,128)S(1)}, f32[1024,1,4]{0,2,1:T(4,128)S(1)}, f32[1024,1,4,128]{0,3,2,1:T(8,128)})) conditional(s32[]{:T(128)} %bitcast.205, (f32[1024,1,4]{0,2,1:T(4,128)S(1)}, f32[1024,1,4]{0,2,1:T(4,128)S(1)}, f32[1024,1,4,128]{0,3,2,1:T(8,128)}) %tuple.164, (s32[]{:T(128)}, f32[1024,1,4]{0,2,1:T(4,128)S(1)}, ...), branch_computations={%region_14.14_spmd, %region_15.17_spmd} | conditional | flops 552356352 | bytes 27172004 | solution.py:86
  416.5 1.9 fusion.41
  420.0 2.3 fusion.51
  423.0 5.7 dynamic_update_slice.31
  438.0 11.7 %conditional.8 = ((f32[1024,1,4]{0,2,1:T(4,128)S(1)}, f32[1024,1,4]{0,2,1:T(4,128)S(1)}, f32[1024,1,4,128]{0,3,2,1:T(8,128)})) conditional(s32[]{:T(128)} %bitcast.205, (f32[1024,1,4]{0,2,1:T(4,128)S(1)}, f32[1024,1,4]{0,2,1:T(4,128)S(1)}, f32[1024,1,4,128]{0,3,2,1:T(8,128)}) %tuple.164, (s32[]{:T(128)}, f32[1024,1,4]{0,2,1:T(4,128)S(1)}, ...), branch_computations={%region_14.14_spmd, %region_15.17_spmd} | conditional | flops 552356352 | bytes 27172004 | solution.py:86
  438.4 1.9 fusion.41
  441.9 2.3 fusion.51
  444.7 5.0 dynamic_update_slice.31
  452.8 11.8 %conditional.8 = ((f32[1024,1,4]{0,2,1:T(4,128)S(1)}, f32[1024,1,4]{0,2,1:T(4,128)S(1)}, f32[1024,1,4,128]{0,3,2,1:T(8,128)})) conditional(s32[]{:T(128)} %bitcast.205, (f32[1024,1,4]{0,2,1:T(4,128)S(1)}, f32[1024,1,4]{0,2,1:T(4,128)S(1)}, f32[1024,1,4,128]{0,3,2,1:T(8,128)}) %tuple.164, (s32[]{:T(128)}, f32[1024,1,4]{0,2,1:T(4,128)S(1)}, ...), branch_computations={%region_14.14_spmd, %region_15.17_spmd} | conditional | flops 552356352 | bytes 27172004 | solution.py:86
  453.2 1.9 fusion.41
  456.7 2.3 fusion.51
  459.5 5.0 dynamic_update_slice.31
  467.6 11.7 %conditional.8 = ((f32[1024,1,4]{0,2,1:T(4,128)S(1)}, f32[1024,1,4]{0,2,1:T(4,128)S(1)}, f32[1024,1,4,128]{0,3,2,1:T(8,128)})) conditional(s32[]{:T(128)} %bitcast.205, (f32[1024,1,4]{0,2,1:T(4,128)S(1)}, f32[1024,1,4]{0,2,1:T(4,128)S(1)}, f32[1024,1,4,128]{0,3,2,1:T(8,128)}) %tuple.164, (s32[]{:T(128)}, f32[1024,1,4]{0,2,1:T(4,128)S(1)}, ...), branch_computations={%region_14.14_spmd, %region_15.17_spmd} | conditional | flops 552356352 | bytes 27172004 | solution.py:86
  468.0 1.9 fusion.41
  471.5 2.3 fusion.51
  474.3 5.0 dynamic_update_slice.31
  482.4 11.8 %conditional.8 = ((f32[1024,1,4]{0,2,1:T(4,128)S(1)}, f32[1024,1,4]{0,2,1:T(4,128)S(1)}, f32[1024,1,4,128]{0,3,2,1:T(8,128)})) conditional(s32[]{:T(128)} %bitcast.205, (f32[1024,1,4]{0,2,1:T(4,128)S(1)}, f32[1024,1,4]{0,2,1:T(4,128)S(1)}, f32[1024,1,4,128]{0,3,2,1:T(8,128)}) %tuple.164, (s32[]{:T(128)}, f32[1024,1,4]{0,2,1:T(4,128)S(1)}, ...), branch_computations={%region_14.14_spmd, %region_15.17_spmd} | conditional | flops 552356352 | bytes 27172004 | solution.py:86
  482.8 1.9 fusion.41
  486.3 2.3 fusion.51
  489.1 5.0 dynamic_update_slice.31
  497.2 11.7 %conditional.8 = ((f32[1024,1,4]{0,2,1:T(4,128)S(1)}, f32[1024,1,4]{0,2,1:T(4,128)S(1)}, f32[1024,1,4,128]{0,3,2,1:T(8,128)})) conditional(s32[]{:T(128)} %bitcast.205, (f32[1024,1,4]{0,2,1:T(4,128)S(1)}, f32[1024,1,4]{0,2,1:T(4,128)S(1)}, f32[1024,1,4,128]{0,3,2,1:T(8,128)}) %tuple.164, (s32[]{:T(128)}, f32[1024,1,4]{0,2,1:T(4,128)S(1)}, ...), branch_computations={%region_14.14_spmd, %region_15.17_spmd} | conditional | flops 552356352 | bytes 27172004 | solution.py:86
  497.6 1.9 fusion.41
  501.1 2.3 fusion.51
  503.9 5.0 dynamic_update_slice.31
  509.1 2.0 copy.26
  511.2 6.3 fusion.69
  517.7 304.5 %psum.7 = f32[32]{0:T(128)S(1)} all-reduce(f32[32]{0:T(128)S(1)} %multiply_dynamic-update-slice_fusion), channel_id=1, replica_groups=mesh['dp'=2,'head'=8,'ctx'=16] {'dp','head','ctx'}, use_global_device_ids=true, to_apply=%region_20.21 | all-reduce | flops 32 | bytes 256 | tf_op jit(solution)/shard_map/psum | solution.py:197
  (520 shorter events, 134.4 us)
Async XLA Ops:
  7.2 20.2 %copy-start.4 = (bf16[1,1024,4,128]{3,2,1,0:T(4,128)(2,1)S(1)}, bf16[1,1024,4,128]{3,2,1,0:T(4,128)(2,1)}, u32[]{:S(2)}) copy-start(bf16[1,1024,4,128]{3,2,1,0:T(4,128)(2,1)} %param.18) | copy-start | bytes 3145732
  7.2 147.5 %all-gather.2.cloned.1.call-start = ((), (), s32[]{:S(2)}) async-start(), calls=%async_computation | async-start | bytes 8912896 | tf_op jit(solution)/shard_map/all_gather | solution.py:141
  9.3 0.8 copy-start.1
  10.1 21.1 %collective-permute-start.1 = (bf16[2,1024,1,128]{3,1,2,0:T(8,128)(2,1)}, bf16[2,1024,1,128]{3,1,2,0:T(8,128)(2,1)S(1)}, u32[]{:S(2)}, u32[]{:S(2)}) collective-permute-start(bf16[2,1024,1,128]{3,1,2,0:T(8,128)(2,1)} %copy-done.1), channel_id=1, source_target_pairs={{0,1},{1,2},{2,3},{3,4},{4,5},{5,6},{6,7},{7,8},{8,9},{9,10},{10,1... | collective-permute-start | bytes 1572872 | tf_op jit(solution)/shard_map/ppermute | solution.py:16
  15.9 39.4 %collective-permute-start = (bf16[2,1024,1,128]{3,1,2,0:T(8,128)(2,1)}, bf16[2,1024,1,128]{3,1,2,0:T(8,128)(2,1)}, u32[]{:S(2)}, u32[]{:S(2)}) collective-permute-start(bf16[2,1024,1,128]{3,1,2,0:T(8,128)(2,1)} %copy-done.1), channel_id=1, source_target_pairs={{0,2},{1,3},{2,4},{3,5},{4,6},{5,7},{6,8},{7,9},{8,10},{9,11},{10,... | collective-permute-start | bytes 1572872 | tf_op jit(solution)/shard_map/ppermute | solution.py:16
  25.8 29.4 %copy-start.2 = (bf16[2,1024,1,128]{3,1,2,0:T(8,128)(2,1)S(1)}, bf16[2,1024,1,128]{3,1,2,0:T(8,128)(2,1)}, u32[]{:S(2)}) copy-start(bf16[2,1024,1,128]{3,1,2,0:T(8,128)(2,1)} %copy-done.1) | copy-start | bytes 1572868
  355.7 1.6 copy-start
  371.4 1.6 copy-start
  387.0 1.6 copy-start
  402.7 1.6 copy-start
  418.4 1.6 copy-start
  440.3 1.6 copy-start
  455.1 1.6 copy-start
  469.9 1.6 copy-start
  484.7 1.6 copy-start
  499.5 1.6 copy-start
  508.9 2.3 copy-start.3
  508.9 2.3 copy-start.6
  511.2 6.4 copy-start.5
Sparse Core Ops, SparseCore 0:
  10.5 144.0 all-gather.1
where the time goes:
time: 836 us; the launch traced here: 829 us
  blocking collectives  304 us (36%)
  local copies, waits for them, and re-layouts  177 us (21%)
  waiting for transfers between devices  123 us (15%)
  loops' own time  119 us (14%)
  matrix products  50 us (6%)
  other arithmetic  27.9 us (3%)
  between operations  14.2 us (2%)
  starting transfers between devices  13.6 us (2%)
    psum x1, blocking collectives, on_device(): totals = lax.psum(padded, ('dp', 'head', 'ctx'))  304 us
    another operation x3, loops' own time, sweep_blocks(): return lax.fori_loop(0, total_steps, visit_block, carried)  117 us
    all_gather x1, waiting for transfers between devices, on_device(): portion = lax.all_gather(stacked, 'ctx', axis=1, tiled=True)  96.1 us
    dynamic_update_slice x39, local copies, waits for them, and re-layouts, compute(): lax.dynamic_update_slice_in_dim(member, fresh_part, row_at, 0)  60.7 us
    slice x66, local copies, waits for them, and re-layouts, visit_block(): row_pos[row_block - 1]  42.8 us
    slice x64, local copies, waits for them, and re-layouts, visit_block(): key_pos[0]  37.7 us
    ppermute x2, waiting for transfers between devices, from_behind(): return lax.ppermute(block, axis, route)  27.2 us
    dot_general x13, matrix products, block_update(): jnp.einsum('rgek,kgh->rgeh', weights.astype(jnp.bfloat16), value_rows, pr...  26.8 us
  transfers between devices with their start and end apart: 3, of which 3 were waited for; matrix products, arithmetic and copies ran while one was open for 1% of the time, Pallas kernels for 0%

commit v1 on v0

v1 whole, which is shorter than its diff:
```python
import functools
import math

import jax
import jax.numpy as jnp
from jax import lax
from jax.experimental import pallas as pl
from jax.experimental.pallas import tpu as pltpu
from jax.sharding import PartitionSpec as P

SINK = 64
WINDOW = 2048
BLOCK = 1024
TILE = 512
DEPTH = 3
LANES = 128
TAIL = 32
VMEM = pltpu.VMEM
LOG2E = 1.4426950408889634
NEG = -1e30


def params():
    return pltpu.CompilerParams(vmem_limit_bytes=48 * 2**20)


def cost(units, bytes_accessed=4 * 2**20):
    return pl.CostEstimate(
        flops=int(units * 4 * BLOCK * BLOCK * LANES),
        bytes_accessed=bytes_accessed,
        transcendentals=int(units * BLOCK * BLOCK),
    )


def scores_of(q, k):
    return lax.dot_general(q, k, (((1,), (1,)), ((), ())), preferred_element_type=jnp.float32)


def fold(carried, scores, values, scale):
    top, total, acc = carried
    newest = jnp.maximum(top, jnp.max(scores, axis=1, keepdims=True) * scale)
    weights = jnp.exp2(scores * scale - newest)
    factor = jnp.exp2(top - newest)
    total = total * factor + jnp.sum(weights, axis=1, keepdims=True)
    acc = acc * factor + jnp.dot(
        weights.astype(jnp.bfloat16), values, preferred_element_type=jnp.float32
    )
    return newest, total, acc


def early_kernel(scale, at, q0, q1, q2, q3, k0, k1, k3, v0, v1, v3, acc_ref, ml_ref, qs, ks, vs):
    index = at[0]
    sets = 4 - index // 4
    for n, ref in enumerate((q0, q1, q2, q3)):
        qs[pl.ds(n * BLOCK, BLOCK), :] = ref[...]
    for n, (kref, vref) in enumerate(((k1, v1), (k3, v3))):
        ks[pl.ds(n * BLOCK, BLOCK), :] = kref[...]
        vs[pl.ds(n * BLOCK, BLOCK), :] = vref[...]
    more = jnp.where(index >= 3, 2, jnp.where(index >= 1, 1, 0))
    row = lax.broadcasted_iota(jnp.int32, (TILE, BLOCK), 0)
    col = lax.broadcasted_iota(jnp.int32, (TILE, BLOCK), 1)
    ahead = col - row

    def tile(t, _):
        rows = pl.ds(pl.multiple_of(t * TILE, TILE), TILE)
        q = qs[rows, :]
        limit = jnp.where(t < BLOCK // TILE, t * TILE, BLOCK)
        scores = jnp.where(ahead <= limit, scores_of(q, k0[...]), NEG)
        start = (
            jnp.full((TILE, 1), NEG, jnp.float32),
            jnp.zeros((TILE, 1), jnp.float32),
            jnp.zeros((TILE, LANES), jnp.float32),
        )
        state = fold(start, scores, v0[...], scale)

        def block(b, carried):
            keys = pl.ds(pl.multiple_of(b * BLOCK, BLOCK), BLOCK)
            return fold(carried, scores_of(q, ks[keys, :]), vs[keys, :], scale)

        top, total, acc = lax.fori_loop(0, more, block, state)
        acc_ref[rows, :] = acc
        lane = lax.broadcasted_iota(jnp.int32, (TILE, LANES), 1)
        ml_ref[rows, :] = jnp.where(lane < LANES // 2, top, total)
        return 0

    lax.fori_loop(0, sets * (BLOCK // TILE), tile, 0)


def late_kernel(scale, at, q0, q1, q2, q3, k2, v2, acc_ref, ml_ref, own_ref, lse_ref, p1, p2, p3, qs, ps, ls):
    index = at[0]
    sets = 4 - index // 4
    for n, ref in enumerate((q0, q1, q2, q3)):
        qs[pl.ds(n * BLOCK, BLOCK), :] = ref[...]

    def tile(t, _):
        rows = pl.ds(pl.multiple_of(t * TILE, TILE), TILE)
        q = qs[rows, :]
        ml = ml_ref[rows, :]
        state = (ml[:, 0:1], ml[:, LANES // 2 : LANES // 2 + 1], acc_ref[rows, :])

        def block(b, carried):
            return fold(carried, scores_of(q, k2[...]), v2[...], scale)

        top, total, acc = lax.fori_loop(0, jnp.where(index >= 2, 1, 0), block, state)
        out = acc / total
        lse = jnp.broadcast_to(top + jnp.log2(total), (TILE, LANES))

        @pl.when(t < BLOCK // TILE)
        def _():
            own_ref[rows, :] = out
            lse_ref[rows, :] = lse

        ps[rows, :] = out.astype(jnp.bfloat16)
        for g in range(TILE // LANES):
            turned = lse[g * LANES : (g + 1) * LANES, :].T
            ls[pl.ds(t * (TILE // LANES) + g, 1), :] = turned[0:1, :]
        return 0

    lax.fori_loop(0, sets * (BLOCK // TILE), tile, 0)
    for n, ref in ((1, p1), (2, p2), (3, p3)):

        @pl.when(n < sets)
        def _():
            ref[0:BLOCK, :] = ps[n * BLOCK : (n + 1) * BLOCK, :]
            value = ls[n * 8 : (n + 1) * 8, :]
            high = value.astype(jnp.bfloat16).astype(jnp.float32)
            rest = value - high
            middle = rest.astype(jnp.bfloat16).astype(jnp.float32)
            ref[BLOCK : BLOCK + TAIL, :] = jnp.concatenate(
                [high, middle, rest - middle, jnp.zeros_like(high)], axis=0
            ).astype(jnp.bfloat16)

        @pl.when(n >= sets)
        def _():
            ref[...] = jnp.zeros_like(ref)


def near_kernel(scale, per_pos, positions, out_dtype, at, q, k0, k1, k2, v0, v1, v2, sinks, out_ref, ks, vs):
    index = at[0]
    for n, (kref, vref) in enumerate(((k2, v2), (k1, v1), (k0, v0))):
        ks[pl.ds(n * BLOCK, BLOCK), :] = kref[...]
        vs[pl.ds(n * BLOCK, BLOCK), :] = vref[...]
    tile = positions * per_pos
    width = WINDOW + positions
    row = lax.broadcasted_iota(jnp.int32, (tile, positions), 0) // per_pos
    col = lax.broadcasted_iota(jnp.int32, (tile, positions), 1)
    sink_row = lax.broadcasted_iota(jnp.int32, (tile, LANES), 0) // per_pos
    sink_col = lax.broadcasted_iota(jnp.int32, (tile, LANES), 1)
    sink_k = sinks[0:LANES, :]
    sink_v = sinks[LANES : 2 * LANES, :]
    first = (2 - index) * BLOCK

    def visit(t, _):
        rows = pl.ds(pl.multiple_of(t * tile, tile), tile)
        begin = pl.multiple_of(t * positions, positions)
        keys = pl.ds(begin, width)
        query = q[rows, :]
        s = scores_of(query, ks[keys, :])
        column = lax.broadcasted_iota(jnp.int32, (1, width), 1) + begin
        s = s + jnp.where(column >= first, 0.0, NEG)
        head = jnp.where(col > row, s[:, :positions], NEG)
        mid = s[:, positions:WINDOW]
        last = jnp.where(col <= row, s[:, WINDOW:], NEG)
        far = scores_of(query, sink_k)
        reach = index * BLOCK + begin + sink_row - sink_col
        far = jnp.where((sink_col < SINK) & (reach >= WINDOW), far, NEG)
        s = jnp.concatenate([head, mid, last, far], axis=1)
        top = jnp.max(s, axis=1, keepdims=True) * scale
        w = jnp.exp2(s * scale - top)
        total = jnp.sum(w, axis=1, keepdims=True)
        w = w.astype(jnp.bfloat16)
        acc = jnp.dot(w[:, :width], vs[keys, :], preferred_element_type=jnp.float32)
        acc = acc + jnp.dot(w[:, width:], sink_v, preferred_element_type=jnp.float32)
        out_ref[rows, :] = (acc / total).astype(out_dtype)
        return 0

    lax.fori_loop(0, BLOCK // positions, visit, 0)


def merge_kernel(norm, at, gate, own, lse, p1, p2, p3, near, grad, mix_ref, row_ref):
    index = at[0]
    spot = at[1]
    level = index // 4
    gated = gate[0]
    terms = []
    for n, ref in ((1, p1), (2, p2), (3, p3)):
        tail = ref[BLOCK : BLOCK + TAIL, :].astype(jnp.float32)
        value = tail[0:8] + tail[8:16] + tail[16:24]
        terms.append(jnp.where(level >= n, value, NEG))
    total = jnp.zeros((1, LANES), jnp.float32)
    for g in range(BLOCK // LANES):
        rows = slice(g * LANES, (g + 1) * LANES)
        logs = [lse[rows, :]]
        for value in terms:
            logs.append(jnp.broadcast_to(value[g : g + 1, :], (LANES, LANES)).T)
        top = functools.reduce(jnp.maximum, logs)
        shares = [jnp.exp2(x - top) for x in logs]
        acc = shares[0] * own[rows, :]
        for share, ref in zip(shares[1:], (p1, p2, p3)):
            acc = acc + share * ref[rows, :].astype(jnp.float32)
        full = acc / functools.reduce(jnp.add, shares)
        close = near[rows, :]
        mix_ref[rows, :] = (gated * full + (1.0 - gated) * close).astype(jnp.bfloat16)
        total = total + jnp.sum(
            grad[rows, :].astype(jnp.float32) * (full - close), axis=0, keepdims=True
        )
    value = jnp.sum(total, axis=1, keepdims=True) * norm
    lane = lax.broadcasted_iota(jnp.int32, row_ref.shape, 1)
    row_ref[...] = jnp.where(lane == spot, value, 0.0)


def call(kernel, scalars, arrays, outs, scratch, estimate):
    specs = [pl.BlockSpec(memory_space=pltpu.SMEM)] * len(scalars)
    specs += [pl.BlockSpec(memory_space=VMEM)] * len(arrays)
    return pl.pallas_call(
        kernel,
        out_shape=outs,
        in_specs=specs,
        out_specs=[pl.BlockSpec(memory_space=VMEM)] * len(outs),
        scratch_shapes=scratch,
        compiler_params=params(),
        cost_estimate=estimate,
    )(*scalars, *arrays)


def shape(rows, dtype):
    return jax.ShapeDtypeStruct((rows, LANES), dtype)


def on_device(query_states, key_states, value_states, gate_values, head_flags, output_grad):
    bf16, f32 = jnp.bfloat16, jnp.float32
    heads = head_flags.shape[0]
    ctx = lax.axis_size("ctx")
    index = lax.axis_index("ctx")
    scale = LOG2E / math.sqrt(LANES)
    keys = key_states.reshape(BLOCK, LANES)
    values = value_states.reshape(BLOCK, LANES)
    marked = (head_flags == 1)[None, :, None]
    which = jnp.sum(head_flags * jnp.arange(heads, dtype=jnp.int32))

    def pick(array):
        return jnp.sum(jnp.where(marked, array[0].astype(f32), 0.0), axis=1).astype(bf16)

    def ring(block, shift):
        return lax.ppermute(block, "ctx", [(i, (i + shift) % ctx) for i in range(ctx)])

    k1, v3 = ring(keys, 1), ring(values, 3)
    v1, k3 = ring(values, 1), ring(keys, 3)
    query = pick(query_states)
    visitors = [
        lax.ppermute(query, "ctx", [(i, i - 4 * n) for i in range(4 * n, ctx)])
        for n in range(1, DEPTH + 1)
    ]
    k2, v2 = ring(k1, 1), ring(v3, -1)
    pad = jnp.zeros((LANES - SINK, LANES), bf16)
    sinks = jnp.concatenate([keys[:SINK], pad, values[:SINK], pad], axis=0)
    reach = ctx
    while reach > 1:
        half = reach // 2
        got = lax.ppermute(sinks, "ctx", [(i, i + half) for i in range(0, ctx, reach)])
        sinks = jnp.where(index % reach == half, got, sinks)
        reach = half
    grad = pick(output_grad)
    at = jnp.stack([index, lax.axis_index("head") * heads + which]).astype(jnp.int32)
    gate = jnp.sum(jnp.where(head_flags == 1, gate_values, 0.0))[None]

    full_rows = (DEPTH + 1) * BLOCK
    acc, ml = call(
        functools.partial(early_kernel, scale),
        [at],
        [query, *visitors, keys, k1, k3, values, v1, v3],
        [shape(full_rows, f32), shape(full_rows, f32)],
        [VMEM((full_rows, LANES), bf16), VMEM((2 * BLOCK, LANES), bf16), VMEM((2 * BLOCK, LANES), bf16)],
        cost(12),
    )
    own, lse, *parts = call(
        functools.partial(late_kernel, scale),
        [at],
        [query, *visitors, k2, v2, acc, ml],
        [shape(BLOCK, f32), shape(BLOCK, f32)] + [shape(BLOCK + TAIL, bf16)] * DEPTH,
        [VMEM((full_rows, LANES), bf16), VMEM((full_rows, LANES), bf16), VMEM((8 * (DEPTH + 1), LANES), f32)],
        cost(4),
    )
    returned = [
        lax.ppermute(part, "ctx", [(i - 4 * n, i) for i in range(4 * n, ctx)])
        for n, part in enumerate(parts, 1)
    ]
    window = [keys, k1, k2, values, v1, v2, sinks]
    scratch = [VMEM((3 * BLOCK, LANES), bf16), VMEM((3 * BLOCK, LANES), bf16)]
    [near_one] = call(
        functools.partial(near_kernel, scale, 1, 256, f32),
        [at],
        [query, *window],
        [shape(BLOCK, f32)],
        scratch,
        cost(2.3),
    )
    [near_all] = call(
        functools.partial(near_kernel, scale, heads, 128, bf16),
        [at],
        [query_states.reshape(BLOCK * heads, LANES), *window],
        [shape(BLOCK * heads, bf16)],
        scratch,
        cost(9),
    )
    norm = 1.0 / math.sqrt(lax.axis_size("dp") * BLOCK * ctx * LANES)
    devices = lax.axis_size("dp") * lax.axis_size("head") * ctx
    mixed, row = call(
        functools.partial(merge_kernel, norm),
        [at, gate],
        [own, lse, *returned, near_one, grad],
        [shape(BLOCK, bf16), shape(devices, f32)],
        [],
        cost(0.1),
    )
    everyone = lax.all_to_all(row, ("dp", "head", "ctx"), 0, 0, tiled=True)
    gate_grad = jnp.sum(everyone, axis=0)[: heads * lax.axis_size("head")]
    near_all = near_all.reshape(1, BLOCK, heads, LANES)
    blended = jnp.where(marked[None], mixed[None, :, None, :], near_all)
    return (blended, gate_grad)


def solution(mesh):
    spec = P("dp", "ctx", "head", None)
    return jax.shard_map(
        on_device,
        mesh=mesh,
        in_specs=(spec, spec, spec, P("head"), P("head"), spec),
        out_specs=(spec, P()),
        check_vma=False,
    )
```

time: 836 us -> 169 us (0.20)
  blocking collectives: 304 us -> 0 us
  local copies, waits for them, and re-layouts: 177 us -> 1.52 us
  loops' own time: 119 us -> 0 us
  waiting for transfers between devices: 123 us -> 31.6 us
  starting transfers between devices: 13.6 us -> 74.1 us
  Pallas kernels: 0 us -> 50.4 us
  matrix products: 50 us -> 0 us
  other arithmetic: 27.9 us -> 9.11 us
  between operations: 14.2 us -> 1.6 us
    psum x1 -> x0, blocking collectives: 304 us -> none  [on_device(): totals = lax.psum(padded, ('dp', 'head', 'ctx'))]
    another operation x81 -> x0, loops' own time: 119 us -> none  [the longest x3 117 us: sweep_blocks(): return lax.fori_loop(0, total_steps, visit_block, carried)]
    all_gather x1 -> x0, waiting for transfers between devices: 96.1 us -> none  [on_device(): portion = lax.all_gather(stacked, 'ctx', axis=1, tiled=True)]
    slice x142 -> x2, local copies, waits for them, and re-layouts: 87.9 us -> 1.49 us  [on_device(): sinks = jnp.concatenate([keys[:SINK], pad, values[:SINK], pad], axis=0)]
    dynamic_update_slice x39 -> x0, local copies, waits for them, and re-layouts: 60.7 us -> none  [compute(): lax.dynamic_update_slice_in_dim(member, fresh_part, row_at, 0)]
    pallas_call x0 -> x5, Pallas kernels: none -> 50.4 us  [call(): pl.pallas_call(kernel, out_shape=outs, in_specs=specs, out_specs=[pl.Bloc...]
    dot_general x26 -> x0, matrix products: 49.3 us -> none  [the longest x13 26.8 us: block_update(): jnp.einsum('rgek,kgh->rgeh', weights.astype(jnp.bfloat16), value_rows, pr...]
    all_to_all x0 -> x1, starting transfers between devices: none -> 33.9 us  [on_device(): everyone = lax.all_to_all(row, ('dp', 'head', 'ctx'), 0, 0, tiled=True)]
  transfers between devices with their start and end apart: 3 -> 17, of which waited for: 3 -> 3; matrix products, arithmetic and copies ran while one was open for 1% -> 5% of each run, Pallas kernels for 0% -> 25%
where the time goes in v1:
time: 169 us; the launch traced here: 168 us
  starting transfers between devices  74.1 us (44%)
  Pallas kernels  50.4 us (30%)
  waiting for transfers between devices  31.6 us (19%)
  other arithmetic  9.11 us (5%)
    pallas_call x5, Pallas kernels, call(): pl.pallas_call(kernel, out_shape=outs, in_specs=specs, out_specs=[pl.Bloc...  50.4 us
    all_to_all x1, starting transfers between devices, on_device(): everyone = lax.all_to_all(row, ('dp', 'head', 'ctx'), 0, 0, tiled=True)  33.9 us
    ppermute x3, waiting for transfers between devices, on_device(): lax.ppermute(query, 'ctx', [(i, i - 4 * n) for i in range(4 * n, ctx)])  19.4 us
    ppermute x4, starting transfers between devices, on_device(): lax.ppermute(sinks, 'ctx', [(i, i + half) for i in range(0, ctx, reach)])  13.4 us
    ppermute x6, starting transfers between devices, ring(): lax.ppermute(block, 'ctx', [(i, (i + shift) % ctx) for i in range(ctx)])  13.2 us
    all_to_all x1, waiting for transfers between devices, on_device(): everyone = lax.all_to_all(row, ('dp', 'head', 'ctx'), 0, 0, tiled=True)  11.4 us
    ppermute x3, starting transfers between devices, on_device(): lax.ppermute(part, 'ctx', [(i - 4 * n, i) for i in range(4 * n, ctx)])  9.74 us
    reduce_sum x1, other arithmetic, pick(): jnp.sum(jnp.where(marked, array[0].astype(f32), 0.0), axis=1).astype(bf16)  4.7 us
  transfers between devices with their start and end apart: 17, of which 3 were waited for; matrix products, arithmetic and copies ran while one was open for 5% of the time, Pallas kernels for 25%

profile of v1, /device:TPU:1, one launch (start us, length us, event | category | flops | bytes accessed | tf_op | source)
XLA Modules:
  0.0 168.4 jit_solution(900451495954235976)
XLA Ops:
  0.6 0.0 copy-start.2
  0.6 0.0 copy-start.1
  0.7 0.0 copy-start.3
  0.7 0.0 copy-start.4
  0.7 0.8 slice_bitcast_fusion
  1.4 0.7 slice_bitcast_fusion.1
  2.2 5.7 %collective-permute-start.12 = (bf16[256,128]{1,0:T(8,128)(2,1)S(1)}, bf16[256,128]{1,0:T(8,128)(2,1)S(1)}, u32[]{:S(2)}, u32[]{:S(2)}) collective-permute-start(bf16[256,128]{1,0:T(8,128)(2,1)S(1)} %pad_maximum_fusion), channel_id=1, source_target_pairs={{0,8},{16,24},{32,40},{48,56},{64,72},{80,88},{96,104},{112,120},{... | collective-permute-start | bytes 196616 | tf_op jit(solution)/shard_map/ppermute | solution.py:260
  7.8 0.7 broadcast_compare_fusion
  8.5 4.7 %fusion = (bf16[1024,128]{1,0:T(8,128)(2,1)S(1)}, bf16[1024,128]{1,0:T(8,128)(2,1)S(1)}) fusion(bf16[1,1024,4,128]{3,2,1,0:T(4,128)(2,1)} %param.11, pred[4]{0:T(512)(128)(4,1)S(1)} %broadcast_compare_fusion, bf16[1,1024,4,128]{3,2,1,0:T(4,128)(2,1)} %param.6), kind=kLoop, calls=%fused_computation.1 | loop fusion | flops 2883584 | bytes 2621444 | tf_op jit(solution)/shard_map/reduce_sum | solution.py:242
  13.2 1.3 collective-permute-start
  14.5 1.3 collective-permute-start.1
  15.8 1.3 collective-permute-start.2
  17.1 0.0 copy-done.2
  17.1 0.1 collective-permute-start.8
  17.2 0.0 collective-permute-done.12
  17.3 3.4 %collective-permute-start.13 = (bf16[256,128]{1,0:T(8,128)(2,1)S(1)}, bf16[256,128]{1,0:T(8,128)(2,1)S(1)}, u32[]{:S(2)}, u32[]{:S(2)}) collective-permute-start(bf16[256,128]{1,0:T(8,128)(2,1)S(1)} %broadcast_select_fusion.1), channel_id=1, source_target_pairs={{0,4},{8,12},{16,20},{24,28},{32,36},{40,44},{48,52},{56,60},{64,6... | collective-permute-start | bytes 196616 | tf_op jit(solution)/shard_map/ppermute | solution.py:260
  20.7 0.0 copy-done.3
  20.7 0.6 multiply_reduce_fusion
  21.9 0.0 collective-permute-done.13
  22.0 3.1 %collective-permute-start.14 = (bf16[256,128]{1,0:T(8,128)(2,1)S(1)}, bf16[256,128]{1,0:T(8,128)(2,1)S(1)}, u32[]{:S(2)}, u32[]{:S(2)}) collective-permute-start(bf16[256,128]{1,0:T(8,128)(2,1)S(1)} %broadcast_select_fusion.2), channel_id=1, source_target_pairs={{0,2},{4,6},{8,10},{12,14},{16,18},{20,22},{24,26},{28,30},{32,34}... | collective-permute-start | bytes 196616 | tf_op jit(solution)/shard_map/ppermute | solution.py:260
  25.1 0.0 copy-done.4
  25.1 0.6 select_reduce_fusion
  25.7 0.7 collective-permute-done.14
  26.4 0.0 collective-permute-start.5
  26.4 0.0 collective-permute-done.q1
  26.4 0.0 copy-done.1
  26.4 3.5 %collective-permute-start.3 = (bf16[1024,128]{1,0:T(8,128)(2,1)S(1)}, bf16[1024,128]{1,0:T(8,128)(2,1)S(1)}, u32[]{:S(2)}, u32[]{:S(2)}) collective-permute-start(bf16[1024,128]{1,0:T(8,128)(2,1)S(1)} %bitcast.23), channel_id=1, source_target_pairs={{0,1},{1,2},{2,3},{3,4},{4,5},{5,6},{6,7},{7,8},{8,9},{9,10},{10,1... | collective-permute-start | bytes 786440 | tf_op jit(solution)/shard_map/ppermute | solution.py:245
  29.9 0.0 collective-permute-done.1.q2
  29.9 3.8 %collective-permute-start.7 = (bf16[1024,128]{1,0:T(8,128)(2,1)S(1)}, bf16[1024,128]{1,0:T(8,128)(2,1)S(1)}, u32[]{:S(2)}, u32[]{:S(2)}) collective-permute-start(bf16[1024,128]{1,0:T(8,128)(2,1)S(1)} %bitcast.24), channel_id=1, source_target_pairs={{0,3},{1,4},{2,5},{3,6},{4,7},{5,8},{6,9},{7,10},{8,11},{9,12},{10... | collective-permute-start | bytes 786440 | tf_op jit(solution)/shard_map/ppermute | solution.py:245
  33.8 0.1 pad_add_fusion.at
  33.8 19.4 %collective-permute-done.2.q3 = bf16[1024,128]{1,0:T(8,128)(2,1)S(1)} collective-permute-done((bf16[1024,128]{1,0:T(8,128)(2,1)S(1)}, bf16[1024,128]{1,0:T(8,128)(2,1)S(1)}, u32[]{:S(2)}, u32[]{:S(2)}) %collective-permute-start.2) | collective-permute-done | bytes 262176 | tf_op jit(solution)/shard_map/ppermute | solution.py:251
  53.2 1.3 collective-permute-start.15
  54.5 0.0 collective-permute-done.3.k1
  54.5 0.1 collective-permute-start.4
  54.6 0.0 collective-permute-done.5.v3
  54.6 5.7 %collective-permute-start.6 = (bf16[1024,128]{1,0:T(8,128)(2,1)S(1)}, bf16[1024,128]{1,0:T(8,128)(2,1)S(1)}, u32[]{:S(2)}, u32[]{:S(2)}) collective-permute-start(bf16[1024,128]{1,0:T(8,128)(2,1)S(1)} %collective-permute-done.5.v3), channel_id=1, source_target_pairs={{0,15},{1,0},{2,1},{3,2},{4,3},{5,4},{6,5},{7,6},{8,7},{9,8},{10,9... | collective-permute-start | bytes 786440 | tf_op jit(solution)/shard_map/ppermute | solution.py:245
  60.3 0.0 collective-permute-done.8.v1
  60.3 0.0 collective-permute-done.7.k3
  60.3 11.5 %shard_map.77 = (f32[4096,128]{1,0:T(8,128)S(1)}, f32[4096,128]{1,0:T(8,128)}) custom-call(s32[2]{0:T(128)S(1)} %pad_add_fusion.at, bf16[1024,128]{1,0:T(8,128)(2,1)S(1)} %get-tuple-element.21.q0.q, bf16[1024,128]{1,0:T(8,128)(2,1)S(1)} %collective-permute-done.q1, bf16[1024,128]{1,0:T(8,128)(2,1)S(1)} %collective-permute-done.1.q2, ...), custom_call_target="tpu_custom_call" | custom-call | flops 6442450944 | bytes 4194304 | tf_op jit(solution)/shard_map/pallas_call | solution.py:215
  71.8 0.0 collective-permute-done.15
  71.8 0.0 collective-permute-done.4.k2
  71.8 0.0 collective-permute-done.6.v2
  71.8 0.0 copy-start
  71.8 5.9 %shard_map.78 = (f32[1024,128]{1,0:T(8,128)S(1)}, f32[1024,128]{1,0:T(8,128)S(1)}, bf16[1056,128]{1,0:T(8,128)(2,1)S(1)}, bf16[1056,128]{1,0:T(8,128)(2,1)S(1)}, bf16[1056,128]{1,0:T(8,128)(2,1)S(1)}) custom-call(s32[2]{0:T(128)S(1)} %pad_add_fusion.at, bf16[1024,128]{1,0:T(8,128)(2,1)S(1)} %get-tuple-element.21.q0.q, ...), custom_call_target="tpu_custom_call" | custom-call | flops 2147483648 | bytes 4194304 | tf_op jit(solution)/shard_map/pallas_call | solution.py:215
  77.7 1.3 collective-permute-start.10
  79.0 1.3 collective-permute-start.11
  80.4 7.1 %collective-permute-start.9 = (bf16[1056,128]{1,0:T(8,128)(2,1)S(1)}, bf16[1056,128]{1,0:T(8,128)(2,1)S(1)}, u32[]{:S(2)}, u32[]{:S(2)}) collective-permute-start(bf16[1056,128]{1,0:T(8,128)(2,1)S(1)} %get-tuple-element.15), channel_id=1, source_target_pairs={{0,4},{1,5},{2,6},{3,7},{4,8},{5,9},{6,10},{7,11},{8,12},{9,13},{1... | collective-permute-start | bytes 811016 | tf_op jit(solution)/shard_map/ppermute | solution.py:285
  87.5 0.0 copy-done
  87.5 24.2 %shard_map.81 = bf16[4096,128]{1,0:T(8,128)(2,1)S(1)} custom-call(s32[2]{0:T(128)S(1)} %pad_add_fusion.at, bf16[4096,128]{1,0:T(8,128)(2,1)S(1)} %bitcast.22, bf16[1024,128]{1,0:T(8,128)(2,1)S(1)} %bitcast.26, bf16[1024,128]{1,0:T(8,128)(2,1)S(1)} %collective-permute-done.3.k1, bf16[1024,128]{1,0:T(8,128)(2,1)S(1)} %collective-permute-done.4.k2, ...), custom_call_target="tpu_custom_call" | custom-call | flops 4831838208 | bytes 4194304 | tf_op jit(solution)/shard_map/pallas_call | solution.py:215
  111.8 6.2 %shard_map.79.near = f32[1024,128]{1,0:T(8,128)S(1)} custom-call(s32[2]{0:T(128)S(1)} %pad_add_fusion.at, bf16[1024,128]{1,0:T(8,128)(2,1)S(1)} %get-tuple-element.21.q0.q, bf16[1024,128]{1,0:T(8,128)(2,1)S(1)} %bitcast.27, bf16[1024,128]{1,0:T(8,128)(2,1)S(1)} %collective-permute-done.3.k1, bf16[1024,128]{1,0:T(8,128)(2,1)S(1)} %collective-permute-done.4.k2, ...), custom_call_target="tpu_custom_call" | custom-call | flops 1234803072 | bytes 4194304 | tf_op jit(solution)/shard_map/pallas_call | solution.py:215
  118.0 0.0 collective-permute-done.10.p2
  118.0 0.0 collective-permute-done.11.p3
  118.0 0.0 collective-permute-done.9.p1
  118.0 2.6 %shard_map.80 = (bf16[1024,128]{1,0:T(8,128)(2,1)S(1)}, f32[256,128]{1,0:T(8,128)}) custom-call(s32[2]{0:T(128)S(1)} %pad_add_fusion.at, f32[1]{0:T(128)} %bitcast.2.gate, f32[1024,128]{1,0:T(8,128)S(1)} %get-tuple-element.13.own, f32[1024,128]{1,0:T(8,128)S(1)} %get-tuple-element.14.lse, bf16[1056,128]{1,0:T(8,128)(2,1)S(1)} %collective-permute-done.9.p1, ...), custom_call_target="tpu_custom_call" | custom-call | flops 53687092 | bytes 4194304 | tf_op jit(solution)/shard_map/pallas_call | solution.py:215
  120.6 33.9 %all-to-all-start = ((f32[256,1,128]{2,1,0:T(1,128)}), f32[256,1,128]{2,1,0:T(1,128)S(1)}, u32[]{:S(2)}, u32[]{:S(2)}) async-start(f32[256,1,128]{2,1,0:T(1,128)} %bitcast.12), calls=%async_computation | async-start | bytes 262144 | tf_op jit(solution)/shard_map/all_to_all | solution.py:316
  154.5 1.6 broadcast_select_fusion
  156.1 11.4 %all-to-all-done = f32[256,1,128]{2,1,0:T(1,128)S(1)} async-done(((f32[256,1,128]{2,1,0:T(1,128)}), f32[256,1,128]{2,1,0:T(1,128)S(1)}, u32[]{:S(2)}, u32[]{:S(2)}) %all-to-all-start) | async-done | bytes 131104 | tf_op jit(solution)/shard_map/all_to_all | solution.py:316
  167.6 0.8 reduce_sum.49
  (6 shorter events, 0.1 us)
Async XLA Ops:
  0.6 16.5 %copy-start.2 = (bf16[1,1024,1,128]{3,1,2,0:T(8,128)(2,1)S(1)}, bf16[1,1024,1,128]{3,1,2,0:T(8,128)(2,1)}, u32[]{:S(2)}) copy-start(bf16[1,1024,1,128]{3,1,2,0:T(8,128)(2,1)} %param.8) | copy-start | bytes 786436
  0.6 25.8 %copy-start.1 = (bf16[1,1024,1,128]{3,1,2,0:T(8,128)(2,1)S(1)}, bf16[1,1024,1,128]{3,1,2,0:T(8,128)(2,1)}, u32[]{:S(2)}) copy-start(bf16[1,1024,1,128]{3,1,2,0:T(8,128)(2,1)} %param.7) | copy-start | bytes 786436
  0.7 20.0 %copy-start.3 = (s32[4]{0:T(128)S(1)}, s32[4]{0:T(128)}, u32[]{:S(2)}) copy-start(s32[4]{0:T(128)} %param.10) | copy-start | bytes 52
  0.7 24.4 %copy-start.4 = (f32[4]{0:T(128)S(1)}, f32[4]{0:T(128)}, u32[]{:S(2)}) copy-start(f32[4]{0:T(128)} %param.9) | copy-start | bytes 52
  2.2 15.1 %collective-permute-start.12 = (bf16[256,128]{1,0:T(8,128)(2,1)S(1)}, bf16[256,128]{1,0:T(8,128)(2,1)S(1)}, u32[]{:S(2)}, u32[]{:S(2)}) collective-permute-start(bf16[256,128]{1,0:T(8,128)(2,1)S(1)} %pad_maximum_fusion), channel_id=1, source_target_pairs={{0,8},{16,24},{32,40},{48,56},{64,72},{80,88},{96,104},{112,120},{... | collective-permute-start | bytes 196616 | tf_op jit(solution)/shard_map/ppermute | solution.py:260
  13.2 13.2 %collective-permute-start = (bf16[1024,128]{1,0:T(8,128)(2,1)S(1)}, bf16[1024,128]{1,0:T(8,128)(2,1)S(1)}, u32[]{:S(2)}, u32[]{:S(2)}) collective-permute-start(bf16[1024,128]{1,0:T(8,128)(2,1)S(1)} %get-tuple-element.21.q0.q), channel_id=1, source_target_pairs={{4,0},{5,1},{6,2},{7,3},{8,4},{9,5},{10,6},{11,7},{12,8},{13,9},{1... | collective-permute-start | bytes 786440 | tf_op jit(solution)/shard_map/ppermute | solution.py:251
  14.5 15.4 %collective-permute-start.1 = (bf16[1024,128]{1,0:T(8,128)(2,1)S(1)}, bf16[1024,128]{1,0:T(8,128)(2,1)S(1)}, u32[]{:S(2)}, u32[]{:S(2)}) collective-permute-start(bf16[1024,128]{1,0:T(8,128)(2,1)S(1)} %get-tuple-element.21.q0.q), channel_id=1, source_target_pairs={{8,0},{9,1},{10,2},{11,3},{12,4},{13,5},{14,6},{15,7},{24,16},{25,... | collective-permute-start | bytes 786440 | tf_op jit(solution)/shard_map/ppermute | solution.py:251
  15.8 37.4 %collective-permute-start.2 = (bf16[1024,128]{1,0:T(8,128)(2,1)S(1)}, bf16[1024,128]{1,0:T(8,128)(2,1)S(1)}, u32[]{:S(2)}, u32[]{:S(2)}) collective-permute-start(bf16[1024,128]{1,0:T(8,128)(2,1)S(1)} %get-tuple-element.21.q0.q), channel_id=1, source_target_pairs={{12,0},{13,1},{14,2},{15,3},{28,16},{29,17},{30,18},{31,19},{44,32... | collective-permute-start | bytes 786440 | tf_op jit(solution)/shard_map/ppermute | solution.py:251
  17.1 43.2 %collective-permute-start.8 = (bf16[1024,128]{1,0:T(8,128)(2,1)S(1)}, bf16[1024,128]{1,0:T(8,128)(2,1)S(1)}, u32[]{:S(2)}, u32[]{:S(2)}) collective-permute-start(bf16[1024,128]{1,0:T(8,128)(2,1)S(1)} %bitcast.28), channel_id=1, source_target_pairs={{0,1},{1,2},{2,3},{3,4},{4,5},{5,6},{6,7},{7,8},{8,9},{9,10},{10,1... | collective-permute-start | bytes 786440 | tf_op jit(solution)/shard_map/ppermute | solution.py:245
  17.3 4.7 %collective-permute-start.13 = (bf16[256,128]{1,0:T(8,128)(2,1)S(1)}, bf16[256,128]{1,0:T(8,128)(2,1)S(1)}, u32[]{:S(2)}, u32[]{:S(2)}) collective-permute-start(bf16[256,128]{1,0:T(8,128)(2,1)S(1)} %broadcast_select_fusion.1), channel_id=1, source_target_pairs={{0,4},{8,12},{16,20},{24,28},{32,36},{40,44},{48,52},{56,60},{64,6... | collective-permute-start | bytes 196616 | tf_op jit(solution)/shard_map/ppermute | solution.py:260
  22.0 4.4 %collective-permute-start.14 = (bf16[256,128]{1,0:T(8,128)(2,1)S(1)}, bf16[256,128]{1,0:T(8,128)(2,1)S(1)}, u32[]{:S(2)}, u32[]{:S(2)}) collective-permute-start(bf16[256,128]{1,0:T(8,128)(2,1)S(1)} %broadcast_select_fusion.2), channel_id=1, source_target_pairs={{0,2},{4,6},{8,10},{12,14},{16,18},{20,22},{24,26},{28,30},{32,34}... | collective-permute-start | bytes 196616 | tf_op jit(solution)/shard_map/ppermute | solution.py:260
  26.4 28.2 %collective-permute-start.5 = (bf16[1024,128]{1,0:T(8,128)(2,1)S(1)}, bf16[1024,128]{1,0:T(8,128)(2,1)S(1)}, u32[]{:S(2)}, u32[]{:S(2)}) collective-permute-start(bf16[1024,128]{1,0:T(8,128)(2,1)S(1)} %bitcast.29), channel_id=1, source_target_pairs={{0,3},{1,4},{2,5},{3,6},{4,7},{5,8},{6,9},{7,10},{8,11},{9,12},{10... | collective-permute-start | bytes 786440 | tf_op jit(solution)/shard_map/ppermute | solution.py:245
  26.4 28.1 %collective-permute-start.3 = (bf16[1024,128]{1,0:T(8,128)(2,1)S(1)}, bf16[1024,128]{1,0:T(8,128)(2,1)S(1)}, u32[]{:S(2)}, u32[]{:S(2)}) collective-permute-start(bf16[1024,128]{1,0:T(8,128)(2,1)S(1)} %bitcast.23), channel_id=1, source_target_pairs={{0,1},{1,2},{2,3},{3,4},{4,5},{5,6},{6,7},{7,8},{8,9},{9,10},{10,1... | collective-permute-start | bytes 786440 | tf_op jit(solution)/shard_map/ppermute | solution.py:245
  29.9 30.3 %collective-permute-start.7 = (bf16[1024,128]{1,0:T(8,128)(2,1)S(1)}, bf16[1024,128]{1,0:T(8,128)(2,1)S(1)}, u32[]{:S(2)}, u32[]{:S(2)}) collective-permute-start(bf16[1024,128]{1,0:T(8,128)(2,1)S(1)} %bitcast.24), channel_id=1, source_target_pairs={{0,3},{1,4},{2,5},{3,6},{4,7},{5,8},{6,9},{7,10},{8,11},{9,12},{10... | collective-permute-start | bytes 786440 | tf_op jit(solution)/shard_map/ppermute | solution.py:245
  53.2 18.6 %collective-permute-start.15 = (bf16[256,128]{1,0:T(8,128)(2,1)S(1)}, bf16[256,128]{1,0:T(8,128)(2,1)S(1)}, u32[]{:S(2)}, u32[]{:S(2)}) collective-permute-start(bf16[256,128]{1,0:T(8,128)(2,1)S(1)} %broadcast_select_fusion.3), channel_id=1, source_target_pairs={{0,1},{2,3},{4,5},{6,7},{8,9},{10,11},{12,13},{14,15},{16,17},{18,... | collective-permute-start | bytes 196616 | tf_op jit(solution)/shard_map/ppermute | solution.py:260
  54.5 17.3 %collective-permute-start.4 = (bf16[1024,128]{1,0:T(8,128)(2,1)S(1)}, bf16[1024,128]{1,0:T(8,128)(2,1)S(1)}, u32[]{:S(2)}, u32[]{:S(2)}) collective-permute-start(bf16[1024,128]{1,0:T(8,128)(2,1)S(1)} %collective-permute-done.3.k1), channel_id=1, source_target_pairs={{0,1},{1,2},{2,3},{3,4},{4,5},{5,6},{6,7},{7,8},{8,9},{9,10},{10,1... | collective-permute-start | bytes 786440 | tf_op jit(solution)/shard_map/ppermute | solution.py:245
  54.6 17.2 %collective-permute-start.6 = (bf16[1024,128]{1,0:T(8,128)(2,1)S(1)}, bf16[1024,128]{1,0:T(8,128)(2,1)S(1)}, u32[]{:S(2)}, u32[]{:S(2)}) collective-permute-start(bf16[1024,128]{1,0:T(8,128)(2,1)S(1)} %collective-permute-done.5.v3), channel_id=1, source_target_pairs={{0,15},{1,0},{2,1},{3,2},{4,3},{5,4},{6,5},{7,6},{8,7},{9,8},{10,9... | collective-permute-start | bytes 786440 | tf_op jit(solution)/shard_map/ppermute | solution.py:245
  71.8 15.7 %copy-start = (bf16[1,1024,4,128]{3,2,1,0:T(4,128)(2,1)S(1)}, bf16[1,1024,4,128]{3,2,1,0:T(4,128)(2,1)}, u32[]{:S(2)}) copy-start(bf16[1,1024,4,128]{3,2,1,0:T(4,128)(2,1)} %param.6) | copy-start | bytes 3145732
  77.7 40.3 %collective-permute-start.10 = (bf16[1056,128]{1,0:T(8,128)(2,1)S(1)}, bf16[1056,128]{1,0:T(8,128)(2,1)S(1)}, u32[]{:S(2)}, u32[]{:S(2)}) collective-permute-start(bf16[1056,128]{1,0:T(8,128)(2,1)S(1)} %get-tuple-element.16), channel_id=1, source_target_pairs={{0,8},{1,9},{2,10},{3,11},{4,12},{5,13},{6,14},{7,15},{16,24},{17,... | collective-permute-start | bytes 811016 | tf_op jit(solution)/shard_map/ppermute | solution.py:285
  79.0 39.0 %collective-permute-start.11 = (bf16[1056,128]{1,0:T(8,128)(2,1)S(1)}, bf16[1056,128]{1,0:T(8,128)(2,1)S(1)}, u32[]{:S(2)}, u32[]{:S(2)}) collective-permute-start(bf16[1056,128]{1,0:T(8,128)(2,1)S(1)} %get-tuple-element.17), channel_id=1, source_target_pairs={{0,12},{1,13},{2,14},{3,15},{16,28},{17,29},{18,30},{19,31},{32,44... | collective-permute-start | bytes 811016 | tf_op jit(solution)/shard_map/ppermute | solution.py:285
  80.4 37.7 %collective-permute-start.9 = (bf16[1056,128]{1,0:T(8,128)(2,1)S(1)}, bf16[1056,128]{1,0:T(8,128)(2,1)S(1)}, u32[]{:S(2)}, u32[]{:S(2)}) collective-permute-start(bf16[1056,128]{1,0:T(8,128)(2,1)S(1)} %get-tuple-element.15), channel_id=1, source_target_pairs={{0,4},{1,5},{2,6},{3,7},{4,8},{5,9},{6,10},{7,11},{8,12},{9,13},{1... | collective-permute-start | bytes 811016 | tf_op jit(solution)/shard_map/ppermute | solution.py:285
  120.6 47.0 %all-to-all-start = ((f32[256,1,128]{2,1,0:T(1,128)}), f32[256,1,128]{2,1,0:T(1,128)S(1)}, u32[]{:S(2)}, u32[]{:S(2)}) async-start(f32[256,1,128]{2,1,0:T(1,128)} %bitcast.12), calls=%async_computation | async-start | bytes 262144 | tf_op jit(solution)/shard_map/all_to_all | solution.py:316
